TPU v7x, 128 devices: a whole 4x4x4 slice. The times are simulated.
128 devices in a mesh: atoms: 16 (over y_hi, z, core), kvec: 8 (over y_lo, x).
Axes of the slice: x: 4, y: 4 (y_hi: 2, y_lo: 2; y = y_hi * 2 + y_lo), z: 4, core: 2. Of those that a mesh axis runs over, the one named last changes fastest.
Arguments:
- positions: float32 [3, 32768], P(None, ('atoms', 'kvec')), may hold values from 0 to 8
- features: bfloat16 [32768, 128], P(('atoms', 'kvec')), may hold values from -6 to 6
- atom_mask: int32 [32768], P(('atoms', 'kvec')), may hold values 0 or 1
- neighbours: int32 [256, 12], P(('atoms', 'kvec')), may hold values from 0 to 255, as said below
- lattice: int32 [3, 12288], P(None, 'kvec'), may hold values from -15 to 15, as said below
- pair_weight: bfloat16 [1024, 128], replicated, may hold values from -0.1875 to 0.1875
- kfilter: float32 [8, 128], replicated, may hold values from -4 to 4
- norm_gain: float32 [128], replicated, may hold values from 0.25 to 1.75
- w_in: bfloat16 [128, 512], replicated, may hold values from -0.5 to 0.5
- w_out: bfloat16 [512, 128], replicated, may hold values from -0.25 to 0.25
Outputs:
- updated: bfloat16 [32768, 128], P(('atoms', 'kvec'))
Inputs may be any that keep to these rules, and one draw needn't show every extreme that they name: `neighbours`: group of a block = its id // 16. The 12 ids of a block are different and each lies in the block's group, the group below or the group above it, cyclically over the 16 groups. `lattice`: the 12288 wavevectors are distinct, none is zero, and no two are negatives of each other.
All inputs are finite; a program needn't handle non-finite values. No bound on the sum of `atom_mask` on one device may be relied on, other than what follows from the above.
Results may differ from a plain program's by a relative error of at most 0.017.
Values may be sent and summed in bfloat16 or wider, within the bound.
A program may use at most 64 MiB of HBM per device.

v0:
```python
import math

import jax
import jax.numpy as jnp
from jax import lax
from jax.experimental import pallas as pl
from jax.experimental.pallas import tpu as pltpu
from jax.sharding import PartitionSpec as P

MESH = pl.DeviceIdType.MESH
F32 = jnp.float32
BF16 = jnp.bfloat16
KW = 12288
BLK = 128
C = 128
KB = 8
KQ = 8
NS = 12
ATOMS = 32768
NT = (((1,), (1,)), ((), ()))

SIN = tuple((-1.0) ** i / math.factorial(2 * i + 1) for i in range(6))
COS = tuple((-1.0) ** i / math.factorial(2 * i) for i in range(7))


def poly(h2, coefs):
    total = h2 * coefs[-1] + coefs[-2]
    for c in coefs[-3::-1]:
        total = total * h2 + c
    return total


def sincos_turns(turns):
    h = (turns - jnp.floor(turns + 0.5)) * math.pi
    h2 = h * h
    s = h * poly(h2, SIN)
    c = poly(h2, COS)
    return 2.0 * s * c, 1.0 - 2.0 * s * s


def kernel(
    pos_ref, feat_ref, mask_ref, nb_ref, lat_ref, pw_ref, kfilter_ref, gain_ref, win_ref, wout_ref,
    out_ref,
    head, feats, tabs, ztab, zm, acc, pres, kft, pbuf, rbuf, gbuf, part, lown, sibs, sibin, lsend, lbuf,
    basis, near, summed, pair,
    g_hs, g_hr, g_fs, g_fr, s_hs, s_hr, s_fs, s_fr, h_s, h_r, x_hs, x_hr, x_fs, x_fr,
    r_s, r_r, a_s, a_r, b_s, b_r, l_s, l_r,
):
    a = lax.axis_index("atoms")
    k = lax.axis_index("kvec")
    core = lax.rem(a, 2)
    g = a // 2
    other = 1 - core
    sib = (g * 2 + other, k)

    def kpeer(d):
        return ((k // 4 + d // 4) % 2) * 4 + (k % 4 + d % 4) % 4

    def gpeer(d):
        return ((g // 4 + d // 4) % 2) * 4 + (g % 4 + d % 4) % 4

    halo_dev = (((g + jnp.where(core == 1, 1, 7)) % 8) * 2 + other, k)

    barrier = pltpu.get_barrier_semaphore()
    for d in range(1, 8):
        pl.semaphore_signal(barrier, inc=1, device_id=(a, kpeer(d)), device_id_type=MESH)
        pl.semaphore_signal(barrier, inc=1, device_id=(gpeer(d) * 2 + core, k), device_id_type=MESH)
    pl.semaphore_signal(barrier, inc=1, device_id=sib, device_id_type=MESH)
    pl.semaphore_signal(barrier, inc=1, device_id=halo_dev, device_id_type=MESH)

    def at_core(c, kk):
        return 16 + c * 16 + 2 * kk

    def at_halo(c, kk):
        return c * 48 + 2 * kk

    own = at_core(core, k)
    lat = lat_ref[:, pl.ds(pl.multiple_of(core * 768, 128), 768)]
    nx, ny, nz = lat[0:1], lat[1:2], lat[2:3]
    bx, by, bz = (jnp.where(n < 0, 1, 0) for n in (nx, ny, nz))
    cls = jnp.where(bx != by, 2, 0) + jnp.where(bx != bz, 1, 0)
    code = ((jnp.abs(nx) * 16 + jnp.abs(ny)) * 64 + cls * 16 + jnp.abs(nz)).astype(F32)
    masked = jnp.transpose(feat_ref[...].astype(F32)) * mask_ref[...].astype(F32)
    for b in range(2):
        head[own + b] = jnp.zeros((8, 128), F32)
        head[own + b, 0:3] = pos_ref[:, b * 128 : (b + 1) * 128]
        for r in range(3):
            at = (b * 3 + r) * 128
            head[own + b, 3 + r : 4 + r] = code[:, at : at + 128]
        feats[own + b] = masked[:, b * 128 : (b + 1) * 128].astype(BF16)
    acc[...] = jnp.zeros_like(acc)
    pres[...] = jnp.zeros_like(pres)
    kft[...] = jnp.transpose(kfilter_ref[...])
    pl.semaphore_wait(barrier, 16)

    def shard(ref, at):
        return ref.at[pl.ds(at, 2)]

    def send(src, dst, ss, rs, dev):
        return pltpu.make_async_remote_copy(
            src_ref=src, dst_ref=dst, send_sem=ss, recv_sem=rs, device_id=dev, device_id_type=MESH
        )

    def group_head(d, kk):
        r = shard(head, at_core(core, kk))
        return send(r, r, g_hs.at[d], g_hr.at[kk], (a, kpeer(d)))

    def group_feat(d, kk):
        r = shard(feats, at_core(core, kk))
        return send(r, r, g_fs.at[d], g_fr.at[kk], (a, kpeer(d)))

    def sib_head(c, kk):
        r = shard(head, at_core(c, kk))
        return send(r, r, s_hs.at[kk], s_hr.at[kk], sib)

    def sib_feat(c, kk):
        r = shard(feats, at_core(c, kk))
        return send(r, r, s_fs.at[kk], s_fr.at[kk], sib)

    def halo(ref, i):
        return send(shard(ref, own), shard(ref, at_halo(other, k)), h_s.at[i], h_r.at[i], halo_dev)

    def halo_in(ref, i):
        r = shard(ref, at_halo(core, k))
        return send(r, r, h_s.at[i], h_r.at[i], halo_dev)

    def spread(ref, d, kk, ss, rs):
        r = shard(ref, at_halo(core, kk))
        return send(r, r, ss.at[d], rs.at[kk], (a, kpeer(d)))

    sib_head(core, k).start()
    sib_feat(core, k).start()
    for d in range(1, 8):
        group_head(d, k).start()
    for d in range(1, 8):
        group_feat(d, k).start()
    halo(head, 0).start()
    halo(feats, 1).start()

    def row_numbers(rows):
        return lax.broadcasted_iota(jnp.int32, (rows, 512), 0)

    numbers = jnp.concatenate(
        [row_numbers(16), row_numbers(8) + 8 * core, 2 * k + lax.rem(row_numbers(8), 2)], axis=0
    ).astype(F32) * 0.125
    xy_rows = lax.broadcasted_iota(jnp.int32, (128, 1536), 0) + 128 * core
    zr = lax.broadcasted_iota(jnp.int32, (16, 1536), 0)
    z_rows = (zr // 2) * 16 + 2 * k + lax.rem(zr, 2)

    def gather_step(kk):
        blocks = [head[at_core(c, kk) + b] for c in range(2) for b in range(2)]
        px, py, pz = (jnp.concatenate([h[i : i + 1] for h in blocks], axis=1) for i in range(3))
        coord = jnp.concatenate(
            [jnp.broadcast_to(py, (16, 512)), jnp.broadcast_to(px, (8, 512)), jnp.broadcast_to(pz, (8, 512))],
            axis=0,
        )
        sines, cosines = sincos_turns(coord * numbers)
        fy = (cosines[0:16], sines[0:16])
        for tx, fx in enumerate((cosines[16:24], sines[16:24])):
            for ix in range(8):
                row = fx[ix : ix + 1]
                for ty in range(2):
                    at = ((tx * 2 + ty) * 8 + ix) * 16
                    tabs[kk, at : at + 16] = (row * fy[ty]).astype(BF16)
        fz = (cosines[24:25], cosines[25:26], sines[24:25], sines[25:26])
        rows = jnp.concatenate([feats[at_core(c, kk) + b] for c in range(2) for b in range(2)], axis=1)
        rows = rows.astype(F32)
        for i in range(4):
            ztab[kk, i : i + 1] = fz[i]
            zm[i * 128 : (i + 1) * 128] = (rows * fz[i]).astype(BF16)
        acc[...] += lax.dot_general(zm[...], tabs[kk], NT, preferred_element_type=F32)
        codes = jnp.concatenate([h[3 + r : 4 + r] for h in blocks for r in range(3)], axis=1).astype(jnp.int32)
        hot_xy = jnp.where((codes // 64) == xy_rows, 1.0, 0.0).astype(BF16)
        hot_z = jnp.where(lax.rem(codes, 64) == z_rows, 1.0, 0.0).astype(BF16)
        pres[...] += lax.dot_general(hot_z, hot_xy, NT, preferred_element_type=F32)

    sib_head(other, k).wait_recv()
    sib_feat(other, k).wait_recv()
    gather_step(k)

    def gather_loop(d, carry):
        kk = kpeer(d)
        group_head(d, kk).wait_recv()
        sib_head(core, kk).start()
        group_feat(d, kk).wait_recv()
        sib_feat(core, kk).start()
        sib_head(other, kk).wait_recv()
        sib_feat(other, kk).wait_recv()
        gather_step(kk)
        return carry

    lax.fori_loop(1, 8, gather_loop, 0)

    def rs_copy(d, src, slot):
        return send(pbuf.at[src], rbuf.at[slot], r_s.at[d], r_r.at[slot], (gpeer(d) * 2 + core, k))

    for d in range(1, 8):
        t = gpeer(d)
        for i in range(4):
            rows = pl.ds(pl.multiple_of(i * 128 + 16 * t, 16), 16)
            pbuf[t, i * 16 : (i + 1) * 16] = acc[rows].astype(BF16)
        rs_copy(d, t, g).start()

    halo_in(head, 0).wait_recv()
    for d in range(1, 8):
        spread(head, d, k, x_hs, x_hr).start()
    halo_in(feats, 1).wait_recv()
    for d in range(1, 8):
        spread(feats, d, k, x_fs, x_fr).start()

    eye = jnp.where(
        lax.broadcasted_iota(jnp.int32, (128, 128), 0) == lax.broadcasted_iota(jnp.int32, (128, 128), 1), 1.0, 0.0
    )

    def pair_step(b):
        me = jnp.transpose(head[own + b])
        mx, my, mz = me[:, 0:1], me[:, 1:2], me[:, 2:3]
        my_block = a * 16 + 2 * k + b

        def one(n, carry):
            ident = nb_ref[b, n]
            at = jnp.clip((ident - (2 * g - 1) * 16 + 256) % 256, 0, 63)
            h = head[at]
            same = jnp.where(ident == my_block, 1.0, 0.0)
            dx, dy, dz = mx - h[0:1], my - h[1:2], mz - h[2:3]
            d2 = dx * dx + dy * dy + dz * dz
            u = jnp.sqrt(d2) * (8.0 / 12.0)
            env = (1.0 - eye * same) * float(NS * BLK) ** -0.5 / (1.0 + d2 * (1.0 / 16.0))
            v = u - 0.5
            level = jnp.exp(v * v * -0.5) * env
            ratio = jnp.exp(u - 4.0)
            cols = pl.ds(pl.multiple_of(n * 128, 128), 128)
            for i in range(KB):
                basis[i * 128 : (i + 1) * 128, cols] = level.astype(BF16)
                if i < KB - 1:
                    level = level * ratio
            near[:, cols] = feats[at]
            return carry

        lax.fori_loop(0, NS, one, 0)
        sums = lax.dot_general(basis[...], near[...], NT, preferred_element_type=F32)
        for i in range(KB):
            scale = math.exp(4.0 * i - 0.5 * i * (i + 1))
            summed[:, i * 128 : (i + 1) * 128] = (sums[i * 128 : (i + 1) * 128] * scale).astype(BF16)
        pair[b * 128 : (b + 1) * 128] = jnp.dot(summed[...], pw_ref[...], preferred_element_type=F32)

    for d in range(1, 8):
        spread(head, d, kpeer(d), x_hs, x_hr).wait_recv()
        spread(feats, d, kpeer(d), x_fs, x_fr).wait_recv()
    pair_step(0)

    for d in range(1, 8):
        rs_copy(d, gpeer(d), gpeer(d)).wait_recv()
    factor = []
    for i in range(4):
        total = acc[pl.ds(pl.multiple_of(i * 128 + 16 * g, 16), 16)]
        for d in range(1, 8):
            total += rbuf[gpeer(d), i * 16 : (i + 1) * 16].astype(F32)
        factor.append(total)

    lane = lax.broadcasted_iota(jnp.int32, (8, 128), 1)
    abs_x = (lane // 16 + 8 * core).astype(F32)
    abs_y = lax.rem(lane, 16).astype(F32)
    kappa = (lax.broadcasted_iota(jnp.int32, (8, 128), 0).astype(F32) + 0.5) * (21.0 / KQ)
    coefs = kft[pl.ds(pl.multiple_of(16 * g, 16), 16)]
    for j in range(2):
        abs_z = (2 * k + j).astype(F32)
        mag = jnp.sqrt(abs_x * abs_x + abs_y * abs_y + abs_z * abs_z) * (2.0 * math.pi / 8.0)
        radial = (mag - kappa) * (KQ / 21.0)
        radial = jnp.exp(radial * radial * -0.5)
        kfilt = jnp.zeros((16, 128), F32)
        for p in range(KQ):
            kfilt += coefs[:, p : p + 1] * radial[p : p + 1]
        kfilt = kfilt * float(ATOMS * KW) ** -0.5

        def f(tz, tx, ty):
            at = (tx * 2 + ty) * 128
            return factor[tz * 2 + j][:, at : at + 128]

        even = (f(0, 0, 0), f(1, 0, 1), f(1, 1, 0), f(0, 1, 1))
        odd = (f(0, 1, 0), f(0, 0, 1), f(1, 0, 0), f(1, 1, 1))
        out_even = [0.0] * 4
        out_odd = [0.0] * 4
        for cl in range(4):
            pxy, pxz = 1.0 - 2.0 * (cl // 2), 1.0 - 2.0 * (cl % 2)
            pyz = pxy * pxz
            weight = pres[cl * 2 + j : cl * 2 + j + 1] * kfilt
            for parts, out, signs in (
                (even, out_even, (1.0, -pyz, -pxz, -pxy)),
                (odd, out_odd, (1.0, pxy, pxz, -pyz)),
            ):
                value = parts[0]
                for s, p in zip(signs[1:], parts[1:]):
                    value = value + p if s > 0 else value - p
                value = value * weight
                for i in range(4):
                    out[i] = out[i] + value if signs[i] > 0 else out[i] - value
        for (tz, tx, ty), value in zip(
            ((0, 0, 0), (1, 0, 1), (1, 1, 0), (0, 1, 1), (0, 1, 0), (0, 0, 1), (1, 0, 0), (1, 1, 1)),
            out_even + out_odd,
        ):
            at = (tx * 2 + ty) * 128
            rows = (tz * 2 + j) * 16
            gbuf[g, rows : rows + 16, at : at + 128] = value.astype(BF16)

    def ag_copy(d, slot):
        return send(gbuf.at[slot], gbuf.at[slot], a_s.at[d], a_r.at[slot], (gpeer(d) * 2 + core, k))

    for d in range(1, 8):
        ag_copy(d, g).start()
    pair_step(1)
    for d in range(1, 8):
        ag_copy(d, gpeer(d)).wait_recv()

    def sib_part(kk):
        return send(sibs.at[kk], sibin.at[kk], b_s.at[kk], b_r.at[kk], sib)

    def own_part(d, src, slot):
        return send(lsend.at[src], lbuf.at[slot], l_s.at[d], l_r.at[slot], (a, kpeer(d)))

    def message(kk):
        values = jnp.dot(gbuf[...].reshape(512, 512), tabs[kk], preferred_element_type=F32)
        fz = [ztab[kk, i : i + 1] for i in range(4)]
        for t in range(8):
            total = values[t * 64 : t * 64 + 16] * fz[0]
            for i in range(1, 4):
                total += values[t * 64 + i * 16 : t * 64 + (i + 1) * 16] * fz[i]
            part[0, t * 16 : (t + 1) * 16] = total[:, 0:256]
            part[1, t * 16 : (t + 1) * 16] = total[:, 256:512]
        lown[kk] = part[core]
        sibs[kk] = part[other].astype(BF16)
        sib_part(kk).start()

    def passed_on(d):
        kk = kpeer(d)
        sib_part(kk).wait_recv()
        lsend[kk] = (lown[kk] + sibin[kk].astype(F32)).astype(BF16)
        own_part(d, kk, k).start()

    message(kpeer(1))

    def message_loop(d, carry):
        message(kpeer(d))
        passed_on(d - 1)
        return carry

    lax.fori_loop(2, 8, message_loop, 0)
    message(k)
    passed_on(7)
    sib_part(k).wait_recv()
    long = lown[k] + sibin[k].astype(F32)
    for d in range(1, 8):
        own_part(d, kpeer(d), kpeer(d)).wait_recv()
        long += lbuf[kpeer(d)].astype(F32)

    total = feat_ref[...].astype(F32) + pair[...] + jnp.transpose(long)
    mean = jnp.mean(total * total, axis=-1, keepdims=True)
    normed = (total * lax.rsqrt(mean + 1e-6) * gain_ref[...]).astype(BF16)
    hidden = jnp.dot(normed, win_ref[...], preferred_element_type=F32)
    hidden = (hidden / (1.0 + jnp.exp(-hidden))).astype(BF16)
    out_ref[...] = (total + jnp.dot(hidden, wout_ref[...], preferred_element_type=F32)).astype(BF16)

    sib_head(core, k).wait_send()
    sib_feat(core, k).wait_send()
    halo(head, 0).wait_send()
    halo(feats, 1).wait_send()
    sib_part(k).wait_send()
    for d in range(1, 8):
        kk = kpeer(d)
        group_head(d, k).wait_send()
        group_feat(d, k).wait_send()
        sib_head(core, kk).wait_send()
        sib_feat(core, kk).wait_send()
        spread(head, d, k, x_hs, x_hr).wait_send()
        spread(feats, d, k, x_fs, x_fr).wait_send()
        rs_copy(d, gpeer(d), g).wait_send()
        ag_copy(d, g).wait_send()
        sib_part(kk).wait_send()
        own_part(d, kk, k).wait_send()


def per_device(positions, features, atom_mask, neighbours, lattice, pair_weight, kfilter, norm_gain, w_in, w_out):
    vmem = pl.BlockSpec(memory_space=pltpu.VMEM)
    smem = pl.BlockSpec(memory_space=pltpu.SMEM)
    dma = pltpu.SemaphoreType.DMA((8,))
    return pl.pallas_call(
        kernel,
        out_shape=jax.ShapeDtypeStruct(features.shape, BF16),
        in_specs=[vmem, vmem, vmem, smem] + [vmem] * 6,
        out_specs=vmem,
        scratch_shapes=[
            pltpu.VMEM((64, 8, 128), F32),
            pltpu.VMEM((64, 128, 128), BF16),
            pltpu.VMEM((8, 512, 512), BF16),
            pltpu.VMEM((8, 8, 512), F32),
            pltpu.VMEM((512, 512), BF16),
            pltpu.VMEM((512, 512), F32),
            pltpu.VMEM((16, 128), F32),
            pltpu.VMEM((128, 8), F32),
            pltpu.VMEM((8, 64, 512), BF16),
            pltpu.VMEM((8, 64, 512), BF16),
            pltpu.VMEM((8, 64, 512), BF16),
            pltpu.VMEM((2, 128, 256), F32),
            pltpu.VMEM((8, 128, 256), F32),
            pltpu.VMEM((8, 128, 256), BF16),
            pltpu.VMEM((8, 128, 256), BF16),
            pltpu.VMEM((8, 128, 256), BF16),
            pltpu.VMEM((8, 128, 256), BF16),
            pltpu.VMEM((1024, 1536), BF16),
            pltpu.VMEM((128, 1536), BF16),
            pltpu.VMEM((128, 1024), BF16),
            pltpu.VMEM((256, 128), F32),
        ]
        + [dma] * 8
        + [pltpu.SemaphoreType.DMA((2,))] * 2
        + [dma] * 12,
        compiler_params=pltpu.CompilerParams(
            collective_id=0, has_side_effects=True, vmem_limit_bytes=48 * 1024 * 1024
        ),
    )(
        positions, features, atom_mask.reshape(1, -1), neighbours, lattice, pair_weight, kfilter,
        norm_gain.reshape(1, -1), w_in, w_out,
    )


def solution(mesh):
    return jax.shard_map(
        per_device,
        mesh=mesh,
        in_specs=(
            P(None, ("atoms", "kvec")),
            P(("atoms", "kvec"), None),
            P(("atoms", "kvec")),
            P(("atoms", "kvec"), None),
            P(None, "kvec"),
            P(),
            P(),
            P(),
            P(),
            P(),
        ),
        out_specs=P(("atoms", "kvec"), None),
        check_vma=False,
    )
```

profile of v0, /device:TPU:1, one launch (start us, length us, event | category | flops | bytes accessed | tf_op | source)
XLA Modules:
  0.0 74.4 jit_solution(7878797256231525320)
XLA Ops:
  0.0 0.0 copy-start.8
  0.0 0.0 copy-start.7
  0.0 0.0 copy-start.9
  0.0 0.7 copy-done.8
  0.7 0.0 copy-done.7
  0.7 0.0 copy-done.9
  0.7 0.0 copy-start
  0.7 0.9 %copy-done = bf16[1024,128]{1,0:T(8,128)(2,1)S(1)} copy-done((bf16[1024,128]{1,0:T(8,128)(2,1)S(1)}, bf16[1024,128]{1,0:T(8,128)(2,1)}, u32[]{:S(2)}) %copy-start) | copy-done | bytes 262168
  1.6 0.0 copy-start.1
  1.7 0.9 %copy-done.1 = bf16[128,512]{1,0:T(8,128)(2,1)S(1)} copy-done((bf16[128,512]{1,0:T(8,128)(2,1)S(1)}, bf16[128,512]{1,0:T(8,128)(2,1)}, u32[]{:S(2)}) %copy-start.1) | copy-done | bytes 131096
  2.6 0.0 copy-start.2
  2.6 0.9 %copy-done.2 = bf16[512,128]{1,0:T(8,128)(2,1)S(1)} copy-done((bf16[512,128]{1,0:T(8,128)(2,1)S(1)}, bf16[512,128]{1,0:T(8,128)(2,1)}, u32[]{:S(2)}) %copy-start.2) | copy-done | bytes 131096
  3.5 0.0 copy-start.3
  3.5 0.8 %copy-done.3 = bf16[256,128]{1,0:T(8,128)(2,1)S(1)} copy-done((bf16[256,128]{1,0:T(8,128)(2,1)S(1)}, bf16[256,128]{1,0:T(8,128)(2,1)}, u32[]{:S(2)}) %copy-start.3) | copy-done | bytes 65560
  4.3 0.0 copy-start.4
  4.3 0.7 copy-done.4
  5.0 0.0 copy-start.5
  5.0 0.7 copy-done.5
  5.7 0.0 copy-start.6
  5.7 0.7 copy-done.6
  6.4 67.3 %shard_map.100 = bf16[256,128]{1,0:T(8,128)(2,1)S(1)} custom-call(f32[3,256]{1,0:T(4,128)S(1)} %copy-done.5, bf16[256,128]{1,0:T(8,128)(2,1)S(1)} %copy-done.3, s32[1,256]{1,0:T(1,128)S(1)} %bitcast.2, s32[2,12]{1,0:T(2,128)S(1)} %copy-done.8, s32[3,1536]{1,0:T(4,128)S(1)} %copy-done.4, bf16[1024,128]{1,0:T(8,128)(2,1)S(1)} %copy-done, ...), custom_call_target="tpu_custom_call" | custom-call | tf_op jit(solution)/shard_map/pallas_call | solution.py:386
  73.8 0.6 copy.12
Async XLA Ops:
  0.0 0.7 copy-start.8
  0.0 0.7 copy-start.7
  0.0 0.7 copy-start.9
  0.7 1.0 %copy-start = (bf16[1024,128]{1,0:T(8,128)(2,1)S(1)}, bf16[1024,128]{1,0:T(8,128)(2,1)}, u32[]{:S(2)}) copy-start(bf16[1024,128]{1,0:T(8,128)(2,1)} %pw_ref.1) | copy-start | bytes 786436
  1.6 0.9 %copy-start.1 = (bf16[128,512]{1,0:T(8,128)(2,1)S(1)}, bf16[128,512]{1,0:T(8,128)(2,1)}, u32[]{:S(2)}) copy-start(bf16[128,512]{1,0:T(8,128)(2,1)} %win_ref.1) | copy-start | bytes 393220
  2.6 0.9 %copy-start.2 = (bf16[512,128]{1,0:T(8,128)(2,1)S(1)}, bf16[512,128]{1,0:T(8,128)(2,1)}, u32[]{:S(2)}) copy-start(bf16[512,128]{1,0:T(8,128)(2,1)} %wout_ref.1) | copy-start | bytes 393220
  3.5 0.8 %copy-start.3 = (bf16[256,128]{1,0:T(8,128)(2,1)S(1)}, bf16[256,128]{1,0:T(8,128)(2,1)}, u32[]{:S(2)}) copy-start(bf16[256,128]{1,0:T(8,128)(2,1)} %feat_ref.1) | copy-start | bytes 196612
  4.3 0.7 copy-start.4
  5.0 0.7 copy-start.5
  5.7 0.7 copy-start.6
where the time goes:
time: 74.7 us; the launch traced here: 74.4 us
  Pallas kernels  67.3 us (90%)
  local copies, waits for them, and re-layouts  7.03 us (9%)
    pallas_call x1, Pallas kernels, per_device(): pl.pallas_call(kernel, out_shape=jax.ShapeDtypeStruct(features.shape, BF1...  67.3 us
    unnamed x21, local copies, waits for them, and re-layouts  7.03 us

commit v1 on v0

v1 whole, which is shorter than its diff:
```python
import math

import jax
import jax.numpy as jnp
from jax import lax
from jax.experimental import pallas as pl
from jax.experimental.pallas import tpu as pltpu
from jax.sharding import PartitionSpec as P

MESH = pl.DeviceIdType.MESH
F32 = jnp.float32
BF16 = jnp.bfloat16
KW = 12288
BLK = 128
C = 128
KB = 8
KQ = 8
NS = 12
ATOMS = 32768
NT = (((1,), (1,)), ((), ()))

SIN = tuple((-1.0) ** i / math.factorial(2 * i + 1) for i in range(6))
COS = tuple((-1.0) ** i / math.factorial(2 * i) for i in range(7))


def poly(h2, coefs):
    total = h2 * coefs[-1] + coefs[-2]
    for c in coefs[-3::-1]:
        total = total * h2 + c
    return total


def sincos_turns(turns):
    h = (turns - jnp.floor(turns + 0.5)) * math.pi
    h2 = h * h
    s = h * poly(h2, SIN)
    c = poly(h2, COS)
    return 2.0 * s * c, 1.0 - 2.0 * s * s


def kernel(
    pos_in, feat_in, mask_in, nb_in, lat_in, pw_in, kfilter_in, gain_in, win_in, wout_in,
    out_ref,
    pos_ref, feat_ref, mask_ref, nb_ref, lat_ref, pw_ref, kfilter_ref, gain_ref, win_ref, wout_ref, in_sem,
    window, stage, tabs, ztab, zm, acc, pres, kft, pbuf, rbuf, gbuf, lown, sibs, sibin, lsend, lbuf,
    basis, near, summed, pair,
    g_s, g_r, s_s, s_r, h_s, h_r, x_s, x_r, r_s, r_r, a_s, a_r, b_s, b_r, l_s, l_r,
):
    a = lax.axis_index("atoms")
    k = lax.axis_index("kvec")
    core = lax.rem(a, 2)
    g = a // 2
    other = 1 - core
    sib = (g * 2 + other, k)

    def kpeer(d):
        return ((k // 4 + d // 4) % 2) * 4 + (k % 4 + d % 4) % 4

    def gpeer(d):
        return ((g // 4 + d // 4) % 2) * 4 + (g % 4 + d % 4) % 4

    halo_dev = (((g + jnp.where(core == 1, 1, 7)) % 8) * 2 + other, k)

    loads = [
        pltpu.make_async_copy(src, dst, in_sem.at[i])
        for i, (src, dst) in enumerate((
            (lat_in, lat_ref), (feat_in, feat_ref), (mask_in, mask_ref), (pos_in, pos_ref), (kfilter_in, kfilter_ref),
            (nb_in, nb_ref), (pw_in, pw_ref), (gain_in, gain_ref), (win_in, win_ref), (wout_in, wout_ref),
        ))
    ]
    barrier = pltpu.get_barrier_semaphore()
    for d in range(1, 8):
        pl.semaphore_signal(barrier, inc=1, device_id=(gpeer(d) * 2 + core, k), device_id_type=MESH)
        pl.semaphore_signal(barrier, inc=1, device_id=(a, kpeer(d)), device_id_type=MESH)
    pl.semaphore_signal(barrier, inc=1, device_id=halo_dev, device_id_type=MESH)
    pl.semaphore_signal(barrier, inc=1, device_id=sib, device_id_type=MESH)
    for load in loads:
        load.start()

    def at_core(c, kk):
        return 16 + c * 16 + 2 * kk

    def at_halo(c, kk):
        return c * 48 + 2 * kk

    own = at_core(core, k)
    acc[...] = jnp.zeros_like(acc)
    pres[...] = jnp.zeros_like(pres)
    for load in loads[:5]:
        load.wait()
    lat = lat_ref[:, pl.ds(pl.multiple_of(core * 768, 128), 768)]
    nx, ny, nz = lat[0:1], lat[1:2], lat[2:3]
    bx, by, bz = (jnp.where(n < 0, 1, 0) for n in (nx, ny, nz))
    cls = jnp.where(bx != by, 2, 0) + jnp.where(bx != bz, 1, 0)
    code_xy = (jnp.abs(nx) * 16 + jnp.abs(ny)).astype(F32)
    code_z = (cls * 16 + jnp.abs(nz)).astype(F32)
    masked = jnp.transpose(feat_ref[...].astype(F32)) * mask_ref[...].astype(F32)
    stage[...] = jnp.zeros_like(stage)
    for b in range(2):
        rest = pos_ref[:, b * 128 : (b + 1) * 128]
        for i in range(3):
            piece = rest.astype(BF16).astype(F32)
            stage[b, 3 * i : 3 * i + 3] = piece
            rest = rest - piece
        for r in range(3):
            at = (b * 3 + r) * 128
            stage[b, 9 + r : 10 + r] = code_xy[:, at : at + 128]
            stage[b, 12 + r : 13 + r] = code_z[:, at : at + 128]
        window[own + b, 0:16] = stage[b].astype(BF16)
        window[own + b, 16:144] = masked[:, b * 128 : (b + 1) * 128].astype(BF16)
    kft[...] = jnp.transpose(kfilter_ref[...])
    pl.semaphore_wait(barrier, 16)

    def half(at, h):
        return window.at[pl.ds(at, 2), pl.ds(80 * h, 80 - 16 * h)]

    def send(src, dst, ss, rs, dev):
        return pltpu.make_async_remote_copy(
            src_ref=src, dst_ref=dst, send_sem=ss, recv_sem=rs, device_id=dev, device_id_type=MESH
        )

    def group_copy(h, d, kk):
        r = half(at_core(core, kk), h)
        return send(r, r, g_s.at[h, d], g_r.at[h, kk], (a, kpeer(d)))

    def sib_copy(h, c, kk):
        r = half(at_core(c, kk), h)
        return send(r, r, s_s.at[h, kk], s_r.at[h, kk], sib)

    def halo_copy(src, dst):
        return send(window.at[pl.ds(src, 2)], window.at[pl.ds(dst, 2)], h_s.at[0], h_r.at[0], halo_dev)

    def spread(d, kk):
        r = window.at[pl.ds(at_halo(core, kk), 2)]
        return send(r, r, x_s.at[d], x_r.at[kk], (a, kpeer(d)))

    for h in range(2):
        for d in (6, 2, 5, 7, 1, 3, 4):
            group_copy(h, d, k).start()
        sib_copy(h, core, k).start()
    halo_copy(own, at_halo(other, k)).start()

    def row_numbers(rows):
        return lax.broadcasted_iota(jnp.int32, (rows, 512), 0)

    numbers = jnp.concatenate(
        [row_numbers(16), row_numbers(8) + 8 * core, 2 * k + lax.rem(row_numbers(8), 2)], axis=0
    ).astype(F32) * 0.125

    def joined(kk, low, count):
        return jnp.concatenate(
            [window[at_core(c, kk) + b, low : low + count] for c in range(2) for b in range(2)], axis=1
        ).astype(F32)

    def tables(kk):
        rows = joined(kk, 0, 16)
        px, py, pz = (rows[i : i + 1] + rows[i + 3 : i + 4] + rows[i + 6 : i + 7] for i in range(3))
        coord = jnp.concatenate(
            [jnp.broadcast_to(py, (16, 512)), jnp.broadcast_to(px, (8, 512)), jnp.broadcast_to(pz, (8, 512))],
            axis=0,
        )
        sines, cosines = sincos_turns(coord * numbers)
        fy = (cosines[0:16], sines[0:16])
        for tx, fx in enumerate((cosines[16:24], sines[16:24])):
            for ix in range(8):
                row = fx[ix : ix + 1]
                for ty in range(2):
                    at = ((tx * 2 + ty) * 8 + ix) * 16
                    tabs[kk, at : at + 16] = (row * fy[ty]).astype(BF16)
        for i, row in enumerate((cosines[24:25], cosines[25:26], sines[24:25], sines[25:26])):
            ztab[kk, i : i + 1] = row

    def factor_step(h, kk):
        rows = joined(kk, 16 + 64 * h, 64)
        for i in range(4):
            zm[i * 64 : (i + 1) * 64] = (rows * ztab[kk, i : i + 1]).astype(BF16)
        acc[h] += lax.dot_general(zm[...], tabs[kk], NT, preferred_element_type=F32)

    def arrive(h, kk):
        group_copy(h, 0, kk).wait_recv()
        sib_copy(h, core, kk).start()

    def use(h, kk):
        sib_copy(h, other, kk).wait_recv()
        if h == 0:
            tables(kk)
        factor_step(h, kk)

    def rs_copy(h, d, src, slot):
        return send(pbuf.at[h, src], rbuf.at[h, slot], r_s.at[h, d], r_r.at[h, slot], (gpeer(d) * 2 + core, k))

    def gather_half(h):
        def step(d, carry):
            arrive(h, kpeer(d))
            use(h, kpeer(d - 1))
            return carry

        lax.fori_loop(1, 8, step, 0)
        use(h, kpeer(7))
        for d in (6, 2, 5, 7, 1, 3, 4):
            t = gpeer(d)
            for i in range(0, 4, 2):
                rows = jnp.concatenate(
                    [acc[h, pl.ds(pl.multiple_of(j * 64 + 8 * t, 8), 8)] for j in (i, i + 1)], axis=0
                )
                pbuf[h, t, i * 8 : i * 8 + 16] = rows.astype(BF16)
            rs_copy(h, d, t, g).start()

    gather_half(0)
    gather_half(1)

    halo_copy(own, at_halo(core, k)).wait_recv()
    for d in (6, 2, 5, 7, 1, 3, 4):
        spread(d, k).start()

    xy_rows = lax.broadcasted_iota(jnp.int32, (128, 512), 0) + 128 * core
    zr = lax.broadcasted_iota(jnp.int32, (16, 512), 0)
    z_rows = ((zr // 2) * 16 + 2 * k + lax.rem(zr, 2)).astype(F32)
    xy_rows = xy_rows.astype(F32)

    def presence_step(kk, carry):
        rows = joined(kk, 0, 16)
        for r in range(3):
            hot_xy = jnp.where(rows[9 + r : 10 + r] == xy_rows, 1.0, 0.0).astype(BF16)
            hot_z = jnp.where(rows[12 + r : 13 + r] == z_rows, 1.0, 0.0).astype(BF16)
            pres[...] += lax.dot_general(hot_z, hot_xy, NT, preferred_element_type=F32)
        return carry

    lax.fori_loop(0, 8, presence_step, 0)

    lane = lax.broadcasted_iota(jnp.int32, (8, 128), 1)
    abs_x = (lane // 16 + 8 * core).astype(F32)
    abs_y = lax.rem(lane, 16).astype(F32)
    kappa = (lax.broadcasted_iota(jnp.int32, (8, 128), 0).astype(F32) + 0.5) * (21.0 / KQ)

    def filter_half(h):
        for d in range(1, 8):
            rs_copy(h, d, gpeer(d), gpeer(d)).wait_recv()
        factor = []
        for i in range(0, 4, 2):
            total = jnp.concatenate(
                [acc[h, pl.ds(pl.multiple_of(j * 64 + 8 * g, 8), 8)] for j in (i, i + 1)], axis=0
            )
            for d in range(1, 8):
                total += rbuf[h, gpeer(d), i * 8 : i * 8 + 16].astype(F32)
            factor += [total[0:8], total[8:16]]
        coefs = kft[pl.ds(pl.multiple_of(64 * h + 8 * g, 8), 8)]
        results = {}
        for j in range(2):
            abs_z = (2 * k + j).astype(F32)
            mag = jnp.sqrt(abs_x * abs_x + abs_y * abs_y + abs_z * abs_z) * (2.0 * math.pi / 8.0)
            radial = (mag - kappa) * (KQ / 21.0)
            radial = jnp.exp(radial * radial * -0.5)
            kfilt = jnp.zeros((8, 128), F32)
            for p in range(KQ):
                kfilt += coefs[:, p : p + 1] * radial[p : p + 1]
            kfilt = kfilt * float(ATOMS * KW) ** -0.5
            names = ((0, 0, 0), (1, 0, 1), (1, 1, 0), (0, 1, 1), (0, 1, 0), (0, 0, 1), (1, 0, 0), (1, 1, 1))
            values = [
                factor[tz * 2 + j][:, (tx * 2 + ty) * 128 : (tx * 2 + ty + 1) * 128] for tz, tx, ty in names
            ]
            even, odd = values[:4], values[4:]
            out_even = [0.0] * 4
            out_odd = [0.0] * 4
            for cl in range(4):
                pxy, pxz = 1.0 - 2.0 * (cl // 2), 1.0 - 2.0 * (cl % 2)
                pyz = pxy * pxz
                weight = pres[cl * 2 + j : cl * 2 + j + 1] * kfilt
                for parts, out, signs in (
                    (even, out_even, (1.0, -pyz, -pxz, -pxy)),
                    (odd, out_odd, (1.0, pxy, pxz, -pyz)),
                ):
                    value = parts[0]
                    for s, p in zip(signs[1:], parts[1:]):
                        value = value + p if s > 0 else value - p
                    value = value * weight
                    for i in range(4):
                        out[i] = out[i] + value if signs[i] > 0 else out[i] - value
            for (tz, tx, ty), value in zip(names, out_even + out_odd):
                results[tz, j, tx, ty] = value
        for tz in range(2):
            for tx in range(2):
                for ty in range(2):
                    at = (tx * 2 + ty) * 128
                    both = jnp.concatenate([results[tz, 0, tx, ty], results[tz, 1, tx, ty]], axis=0)
                    gbuf[h, g, tz * 16 : tz * 16 + 16, at : at + 128] = both.astype(BF16)
        for d in (6, 2, 5, 7, 1, 3, 4):
            ag_copy(h, d, g).start()

    def ag_copy(h, d, slot):
        r = gbuf.at[h, slot]
        return send(r, r, a_s.at[h, d], a_r.at[h, slot], (gpeer(d) * 2 + core, k))

    eye = jnp.where(
        lax.broadcasted_iota(jnp.int32, (128, 128), 0) == lax.broadcasted_iota(jnp.int32, (128, 128), 1), 1.0, 0.0
    )

    def pair_step(b):
        me = jnp.transpose(window[own + b, 0:16].astype(F32))
        mx, my, mz = (me[:, i : i + 1] + me[:, i + 3 : i + 4] + me[:, i + 6 : i + 7] for i in range(3))
        my_block = a * 16 + 2 * k + b

        def one(n, carry):
            ident = nb_ref[b, n]
            at = jnp.clip((ident - (2 * g - 1) * 16 + 256) % 256, 0, 63)
            r = window[at, 0:16].astype(F32)
            px, py, pz = (r[i : i + 1] + r[i + 3 : i + 4] + r[i + 6 : i + 7] for i in range(3))
            same = jnp.where(ident == my_block, 1.0, 0.0)
            dx, dy, dz = mx - px, my - py, mz - pz
            d2 = dx * dx + dy * dy + dz * dz
            u = jnp.sqrt(d2) * (8.0 / 12.0)
            env = (1.0 - eye * same) * float(NS * BLK) ** -0.5 / (1.0 + d2 * (1.0 / 16.0))
            v = u - 0.5
            level = jnp.exp(v * v * -0.5) * env
            ratio = jnp.exp(u - 4.0)
            cols = pl.ds(pl.multiple_of(n * 128, 128), 128)
            for i in range(KB):
                basis[i * 128 : (i + 1) * 128, cols] = level.astype(BF16)
                if i < KB - 1:
                    level = level * ratio
            near[:, cols] = window[at, 16:144]
            return carry

        lax.fori_loop(0, NS, one, 0)
        sums = lax.dot_general(basis[...], near[...], NT, preferred_element_type=F32)
        for i in range(KB):
            scale = math.exp(4.0 * i - 0.5 * i * (i + 1))
            summed[:, i * 128 : (i + 1) * 128] = (sums[i * 128 : (i + 1) * 128] * scale).astype(BF16)
        pair[b * 128 : (b + 1) * 128] = jnp.dot(summed[...], pw_ref[...], preferred_element_type=F32)

    filter_half(0)
    filter_half(1)
    for load in loads[5:7]:
        load.wait()
    for d in range(1, 8):
        spread(d, kpeer(d)).wait_recv()
    pair_step(0)

    def sib_part(h, kk):
        return send(sibs.at[h, kk], sibin.at[h, kk], b_s.at[h, kk], b_r.at[h, kk], sib)

    def own_part(h, d, src, slot):
        return send(lsend.at[h, src], lbuf.at[h, slot], l_s.at[h, d], l_r.at[h, slot], (a, kpeer(d)))

    def message(h, kk):
        values = jnp.dot(gbuf[h].reshape(256, 512), tabs[kk], preferred_element_type=F32)
        fz = [ztab[kk, i : i + 1] for i in range(4)]
        for t in range(0, 8, 2):
            pieces = []
            for u in (t, t + 1):
                total = values[u * 32 : u * 32 + 8] * fz[0]
                for i in range(1, 4):
                    total += values[u * 32 + i * 8 : u * 32 + (i + 1) * 8] * fz[i]
                pieces.append(total)
            both = jnp.concatenate(pieces, axis=0)
            low, high = both[:, 0:256], both[:, 256:512]
            lown[h, kk, t * 8 : t * 8 + 16] = jnp.where(core == 0, low, high)
            sibs[h, kk, t * 8 : t * 8 + 16] = jnp.where(core == 0, high, low).astype(BF16)
        sib_part(h, kk).start()

    def passed_on(h, d):
        kk = kpeer(d)
        sib_part(h, kk).wait_recv()
        lsend[h, kk] = (lown[h, kk] + sibin[h, kk].astype(F32)).astype(BF16)
        own_part(h, d, kk, k).start()

    for h in range(2):
        for d in range(1, 8):
            ag_copy(h, d, gpeer(d)).wait_recv()
        message(h, kpeer(7))
        message(h, kpeer(6))

        def message_loop(i, carry):
            message(h, kpeer(7 - i))
            passed_on(h, 9 - i)
            return carry

        lax.fori_loop(2, 7, message_loop, 0)
        message(h, k)
        passed_on(h, 2)
        passed_on(h, 1)

    pair_step(1)
    rest = feat_ref[...].astype(F32) + pair[...]
    for load in loads[7:]:
        load.wait()
    longs = []
    for h in range(2):
        sib_part(h, k).wait_recv()
        long = lown[h, k] + sibin[h, k].astype(F32)
        for d in range(1, 8):
            own_part(h, d, kpeer(d), kpeer(d)).wait_recv()
            long += lbuf[h, kpeer(d)].astype(F32)
        longs.append(long)

    total = rest + jnp.transpose(jnp.concatenate(longs, axis=0))
    mean = jnp.mean(total * total, axis=-1, keepdims=True)
    normed = (total * lax.rsqrt(mean + 1e-6) * gain_ref[...]).astype(BF16)
    hidden = jnp.dot(normed, win_ref[...], preferred_element_type=F32)
    hidden = (hidden / (1.0 + jnp.exp(-hidden))).astype(BF16)
    out_ref[...] = (total + jnp.dot(hidden, wout_ref[...], preferred_element_type=F32)).astype(BF16)

    halo_copy(own, at_halo(other, k)).wait_send()
    for h in range(2):
        sib_copy(h, core, k).wait_send()
        sib_part(h, k).wait_send()
        for d in range(1, 8):
            kk = kpeer(d)
            group_copy(h, d, k).wait_send()
            sib_copy(h, core, kk).wait_send()
            rs_copy(h, d, gpeer(d), g).wait_send()
            ag_copy(h, d, g).wait_send()
            sib_part(h, kk).wait_send()
            own_part(h, d, kk, k).wait_send()
    for d in range(1, 8):
        spread(d, k).wait_send()


def per_device(positions, features, atom_mask, neighbours, lattice, pair_weight, kfilter, norm_gain, w_in, w_out):
    dma = pltpu.SemaphoreType.DMA((2, 8))
    operands = (
        positions, features, atom_mask.reshape(1, -1), neighbours, lattice, pair_weight, kfilter,
        norm_gain.reshape(1, -1), w_in, w_out,
    )
    return pl.pallas_call(
        kernel,
        out_shape=jax.ShapeDtypeStruct(features.shape, BF16),
        in_specs=[pl.BlockSpec(memory_space=pl.ANY)] * len(operands),
        out_specs=pl.BlockSpec(memory_space=pltpu.VMEM),
        scratch_shapes=[
            (pltpu.SMEM if x is neighbours else pltpu.VMEM)(x.shape, x.dtype) for x in operands
        ]
        + [
            pltpu.SemaphoreType.DMA((10,)),
            pltpu.VMEM((64, 144, 128), BF16),
            pltpu.VMEM((2, 16, 128), F32),
            pltpu.VMEM((8, 512, 512), BF16),
            pltpu.VMEM((8, 8, 512), F32),
            pltpu.VMEM((256, 512), BF16),
            pltpu.VMEM((2, 256, 512), F32),
            pltpu.VMEM((16, 128), F32),
            pltpu.VMEM((128, 8), F32),
            pltpu.VMEM((2, 8, 32, 512), BF16),
            pltpu.VMEM((2, 8, 32, 512), BF16),
            pltpu.VMEM((2, 8, 32, 512), BF16),
            pltpu.VMEM((2, 8, 64, 256), F32),
            pltpu.VMEM((2, 8, 64, 256), BF16),
            pltpu.VMEM((2, 8, 64, 256), BF16),
            pltpu.VMEM((2, 8, 64, 256), BF16),
            pltpu.VMEM((2, 8, 64, 256), BF16),
            pltpu.VMEM((1024, 1536), BF16),
            pltpu.VMEM((128, 1536), BF16),
            pltpu.VMEM((128, 1024), BF16),
            pltpu.VMEM((256, 128), F32),
        ]
        + [dma] * 4
        + [pltpu.SemaphoreType.DMA((1,))] * 2
        + [pltpu.SemaphoreType.DMA((8,))] * 2
        + [dma] * 8,
        compiler_params=pltpu.CompilerParams(
            collective_id=0, has_side_effects=True, vmem_limit_bytes=56 * 1024 * 1024
        ),
    )(*operands)


def solution(mesh):
    return jax.shard_map(
        per_device,
        mesh=mesh,
        in_specs=(
            P(None, ("atoms", "kvec")),
            P(("atoms", "kvec"), None),
            P(("atoms", "kvec")),
            P(("atoms", "kvec"), None),
            P(None, "kvec"),
            P(),
            P(),
            P(),
            P(),
            P(),
        ),
        out_specs=P(("atoms", "kvec"), None),
        check_vma=False,
    )
```

time: 74.7 us -> 57.6 us (0.77)
  Pallas kernels: 67.3 us -> 55.9 us
  local copies, waits for them, and re-layouts: 7.03 us -> 1.47 us
    pallas_call x1, Pallas kernels: 67.3 us -> 55.9 us  [per_device(): pl.pallas_call(kernel, out_shape=jax.ShapeDtypeStruct(features.shape, BF1...]
    unnamed x21 -> x1, local copies, waits for them, and re-layouts: 7.03 us -> 1.47 us
where the time goes in v1:
time: 57.6 us; the launch traced here: 57.4 us
  Pallas kernels  55.9 us (97%)
  local copies, waits for them, and re-layouts  1.47 us (3%)
    pallas_call x1, Pallas kernels, per_device(): pl.pallas_call(kernel, out_shape=jax.ShapeDtypeStruct(features.shape, BF1...  55.9 us
    unnamed x1, local copies, waits for them, and re-layouts  1.47 us

profile of v1, /device:TPU:1, one launch (start us, length us, event | category | flops | bytes accessed | tf_op | source)
XLA Modules:
  0.0 57.4 jit_solution(5163737026922961629)
XLA Ops:
  0.0 55.9 %shard_map.100 = bf16[256,128]{1,0:T(8,128)(2,1)} custom-call(f32[3,256]{1,0:T(4,128)} %pos_in.1, bf16[256,128]{1,0:T(8,128)(2,1)} %feat_in.1, s32[1,256]{1,0:T(1,128)} %bitcast.2, s32[2,12]{1,0:T(2,128)} %nb_in.1, s32[3,1536]{1,0:T(4,128)} %lat_in.1, bf16[1024,128]{1,0:T(8,128)(2,1)} %pw_in.1, f32[8,128]{1,0:T(8,128)} %kfilter_in.1, f32[1,128]{1,0:T(1,128)} %bitcast.3, ...), custom_call_target="tpu_custom_call" | custom-call | tf_op jit(solution)/shard_map/pallas_call | solution.py:425
  55.9 1.5 %copy.12 = bf16[256,128]{1,0:T(8,128)(2,1)} copy(bf16[256,128]{1,0:T(8,128)(2,1)} %shard_map.100) | data formatting | bytes 131072

commit v2 on v1

--- a/solution.py
+++ b/solution.py
@@ -130,15 +130,18 @@
     def halo_copy(src, dst):
         return send(window.at[pl.ds(src, 2)], window.at[pl.ds(dst, 2)], h_s.at[0], h_r.at[0], halo_dev)
 
+    ky = (k + 4) % 8
+
     def spread(d, kk):
         r = window.at[pl.ds(at_halo(core, kk), 2)]
-        return send(r, r, x_s.at[d], x_r.at[kk], (a, kpeer(d)))
-
-    for h in range(2):
-        for d in (6, 2, 5, 7, 1, 3, 4):
-            group_copy(h, d, k).start()
-        sib_copy(h, core, k).start()
+        at = d - 1 if kk is k else d + 3
+        return send(r, r, x_s.at[at], x_r.at[kk], (a, kpeer(d)))
+
+    sib_copy(0, core, k).start()
+    for d in range(1, 8):
+        group_copy(0, d, k).start()
     halo_copy(own, at_halo(other, k)).start()
+    sib_copy(1, core, k).start()
 
     def row_numbers(rows):
         return lax.broadcasted_iota(jnp.int32, (rows, 512), 0)
@@ -176,9 +179,12 @@
             zm[i * 64 : (i + 1) * 64] = (rows * ztab[kk, i : i + 1]).astype(BF16)
         acc[h] += lax.dot_general(zm[...], tabs[kk], NT, preferred_element_type=F32)
 
-    def arrive(h, kk):
+    def arrive(h, d):
+        kk = kpeer(d)
         group_copy(h, 0, kk).wait_recv()
         sib_copy(h, core, kk).start()
+        if h == 0:
+            group_copy(1, d, k).start()
 
     def use(h, kk):
         sib_copy(h, other, kk).wait_recv()
@@ -191,7 +197,7 @@
 
     def gather_half(h):
         def step(d, carry):
-            arrive(h, kpeer(d))
+            arrive(h, d)
             use(h, kpeer(d - 1))
             return carry
 
@@ -209,8 +215,9 @@
     gather_half(0)
     gather_half(1)
 
+
     halo_copy(own, at_halo(core, k)).wait_recv()
-    for d in (6, 2, 5, 7, 1, 3, 4):
+    for d in (4, 1, 3, 2):
         spread(d, k).start()
 
     xy_rows = lax.broadcasted_iota(jnp.int32, (128, 512), 0) + 128 * core
@@ -300,7 +307,7 @@
         mx, my, mz = (me[:, i : i + 1] + me[:, i + 3 : i + 4] + me[:, i + 6 : i + 7] for i in range(3))
         my_block = a * 16 + 2 * k + b
 
-        def one(n, carry):
+        def one(n):
             ident = nb_ref[b, n]
             at = jnp.clip((ident - (2 * g - 1) * 16 + 256) % 256, 0, 63)
             r = window[at, 0:16].astype(F32)
@@ -308,33 +315,41 @@
             same = jnp.where(ident == my_block, 1.0, 0.0)
             dx, dy, dz = mx - px, my - py, mz - pz
             d2 = dx * dx + dy * dy + dz * dz
-            u = jnp.sqrt(d2) * (8.0 / 12.0)
+            u = d2 * lax.rsqrt(jnp.maximum(d2, 1e-30)) * (8.0 / 12.0)
             env = (1.0 - eye * same) * float(NS * BLK) ** -0.5 / (1.0 + d2 * (1.0 / 16.0))
             v = u - 0.5
             level = jnp.exp(v * v * -0.5) * env
             ratio = jnp.exp(u - 4.0)
-            cols = pl.ds(pl.multiple_of(n * 128, 128), 128)
+            cols = slice(n * 128, (n + 1) * 128)
             for i in range(KB):
                 basis[i * 128 : (i + 1) * 128, cols] = level.astype(BF16)
                 if i < KB - 1:
                     level = level * ratio
             near[:, cols] = window[at, 16:144]
-            return carry
-
-        lax.fori_loop(0, NS, one, 0)
-        sums = lax.dot_general(basis[...], near[...], NT, preferred_element_type=F32)
+
+        def product(p):
+            cols = slice(p * 256, (p + 1) * 256)
+            return lax.dot_general(basis[:, cols], near[:, cols], NT, preferred_element_type=F32)
+
+        sums = 0.0
+        for p in range(NS // 2):
+            one(2 * p)
+            one(2 * p + 1)
+            if p:
+                sums = sums + product(p - 1)
+        sums = sums + product(NS // 2 - 1)
         for i in range(KB):
             scale = math.exp(4.0 * i - 0.5 * i * (i + 1))
             summed[:, i * 128 : (i + 1) * 128] = (sums[i * 128 : (i + 1) * 128] * scale).astype(BF16)
         pair[b * 128 : (b + 1) * 128] = jnp.dot(summed[...], pw_ref[...], preferred_element_type=F32)
 
     filter_half(0)
+    spread(4, ky).wait_recv()
+    for d in (1, 3, 2):
+        spread(d, ky).start()
     filter_half(1)
     for load in loads[5:7]:
         load.wait()
-    for d in range(1, 8):
-        spread(d, kpeer(d)).wait_recv()
-    pair_step(0)
 
     def sib_part(h, kk):
         return send(sibs.at[h, kk], sibin.at[h, kk], b_s.at[h, kk], b_r.at[h, kk], sib)
@@ -380,6 +395,9 @@
         passed_on(h, 2)
         passed_on(h, 1)
 
+    for d in (1, 2, 3, 5, 6, 7):
+        spread(d, kpeer(d)).wait_recv()
+    pair_step(0)
     pair_step(1)
     rest = feat_ref[...].astype(F32) + pair[...]
     for load in loads[7:]:
@@ -412,8 +430,10 @@
             ag_copy(h, d, g).wait_send()
             sib_part(h, kk).wait_send()
             own_part(h, d, kk, k).wait_send()
-    for d in range(1, 8):
+    spread(4, k).wait_send()
+    for d in range(1, 4):
         spread(d, k).wait_send()
+        spread(d, ky).wait_send()
 
 
 def per_device(positions, features, atom_mask, neighbours, lattice, pair_weight, kfilter, norm_gain, w_in, w_out):

time: 57.6 us -> 51.2 us (0.89)
  Pallas kernels: 55.9 us -> 49.5 us
    pallas_call x1, Pallas kernels: 55.9 us -> 49.5 us  [per_device(): pl.pallas_call(kernel, out_shape=jax.ShapeDtypeStruct(features.shape, BF1...]
where the time goes in v2:
time: 51.2 us; the launch traced here: 51 us
  Pallas kernels  49.5 us (97%)
  local copies, waits for them, and re-layouts  1.47 us (3%)
    pallas_call x1, Pallas kernels, per_device(): pl.pallas_call(kernel, out_shape=jax.ShapeDtypeStruct(features.shape, BF1...  49.5 us
    unnamed x1, local copies, waits for them, and re-layouts  1.47 us

profile of v2, /device:TPU:1, one launch (start us, length us, event | category | flops | bytes accessed | tf_op | source)
XLA Modules:
  0.0 51.0 jit_solution(10586990211933658826)
XLA Ops:
  0.0 49.5 %shard_map.100 = bf16[256,128]{1,0:T(8,128)(2,1)} custom-call(f32[3,256]{1,0:T(4,128)} %pos_in.1, bf16[256,128]{1,0:T(8,128)(2,1)} %feat_in.1, s32[1,256]{1,0:T(1,128)} %bitcast.2, s32[2,12]{1,0:T(2,128)} %nb_in.1, s32[3,1536]{1,0:T(4,128)} %lat_in.1, bf16[1024,128]{1,0:T(8,128)(2,1)} %pw_in.1, f32[8,128]{1,0:T(8,128)} %kfilter_in.1, f32[1,128]{1,0:T(1,128)} %bitcast.3, ...), custom_call_target="tpu_custom_call" | custom-call | tf_op jit(solution)/shard_map/pallas_call | solution.py:445
  49.5 1.5 %copy.12 = bf16[256,128]{1,0:T(8,128)(2,1)} copy(bf16[256,128]{1,0:T(8,128)(2,1)} %shard_map.100) | data formatting | bytes 131072

commit v3 on v2

--- a/solution.py
+++ b/solution.py
@@ -196,12 +196,15 @@
         return send(pbuf.at[h, src], rbuf.at[h, slot], r_s.at[h, d], r_r.at[h, slot], (gpeer(d) * 2 + core, k))
 
     def gather_half(h):
+        arrive(h, 1)
+
         def step(d, carry):
             arrive(h, d)
-            use(h, kpeer(d - 1))
+            use(h, kpeer(d - 2))
             return carry
 
-        lax.fori_loop(1, 8, step, 0)
+        lax.fori_loop(2, 8, step, 0)
+        use(h, kpeer(6))
         use(h, kpeer(7))
         for d in (6, 2, 5, 7, 1, 3, 4):
             t = gpeer(d)
@@ -215,10 +218,6 @@
     gather_half(0)
     gather_half(1)
 
-
-    halo_copy(own, at_halo(core, k)).wait_recv()
-    for d in (4, 1, 3, 2):
-        spread(d, k).start()
 
     xy_rows = lax.broadcasted_iota(jnp.int32, (128, 512), 0) + 128 * core
     zr = lax.broadcasted_iota(jnp.int32, (16, 512), 0)
@@ -344,10 +343,13 @@
         pair[b * 128 : (b + 1) * 128] = jnp.dot(summed[...], pw_ref[...], preferred_element_type=F32)
 
     filter_half(0)
+    halo_copy(own, at_halo(core, k)).wait_recv()
+    for d in (4, 1, 3, 2):
+        spread(d, k).start()
+    filter_half(1)
     spread(4, ky).wait_recv()
     for d in (1, 3, 2):
         spread(d, ky).start()
-    filter_half(1)
     for load in loads[5:7]:
         load.wait()
 
@@ -384,15 +386,17 @@
             ag_copy(h, d, gpeer(d)).wait_recv()
         message(h, kpeer(7))
         message(h, kpeer(6))
+        message(h, kpeer(5))
 
         def message_loop(i, carry):
             message(h, kpeer(7 - i))
-            passed_on(h, 9 - i)
+            passed_on(h, 10 - i)
             return carry
 
-        lax.fori_loop(2, 7, message_loop, 0)
+        lax.fori_loop(3, 7, message_loop, 0)
+        passed_on(h, 3)
+        passed_on(h, 2)
         message(h, k)
-        passed_on(h, 2)
         passed_on(h, 1)
 
     for d in (1, 2, 3, 5, 6, 7):

time: 51.2 us -> 48 us (0.938)
  Pallas kernels: 49.5 us -> 46.3 us
    pallas_call x1, Pallas kernels: 49.5 us -> 46.3 us  [per_device(): pl.pallas_call(kernel, out_shape=jax.ShapeDtypeStruct(features.shape, BF1...]
where the time goes in v3:
time: 48 us; the launch traced here: 47.8 us
  Pallas kernels  46.3 us (96%)
  local copies, waits for them, and re-layouts  1.47 us (3%)
    pallas_call x1, Pallas kernels, per_device(): pl.pallas_call(kernel, out_shape=jax.ShapeDtypeStruct(features.shape, BF1...  46.3 us
    unnamed x1, local copies, waits for them, and re-layouts  1.47 us

profile of v3, /device:TPU:1, one launch (start us, length us, event | category | flops | bytes accessed | tf_op | source)
XLA Modules:
  0.0 47.8 jit_solution(1829075057203380902)
XLA Ops:
  0.0 46.3 %shard_map.100 = bf16[256,128]{1,0:T(8,128)(2,1)} custom-call(f32[3,256]{1,0:T(4,128)} %pos_in.1, bf16[256,128]{1,0:T(8,128)(2,1)} %feat_in.1, s32[1,256]{1,0:T(1,128)} %bitcast.2, s32[2,12]{1,0:T(2,128)} %nb_in.1, s32[3,1536]{1,0:T(4,128)} %lat_in.1, bf16[1024,128]{1,0:T(8,128)(2,1)} %pw_in.1, f32[8,128]{1,0:T(8,128)} %kfilter_in.1, f32[1,128]{1,0:T(1,128)} %bitcast.3, ...), custom_call_target="tpu_custom_call" | custom-call | tf_op jit(solution)/shard_map/pallas_call | solution.py:449
  46.3 1.5 %copy.12 = bf16[256,128]{1,0:T(8,128)(2,1)} copy(bf16[256,128]{1,0:T(8,128)(2,1)} %shard_map.100) | data formatting | bytes 131072
